TPU v7x, 512 devices: a whole 4x4x16 slice. The times are simulated.
512 devices in a mesh: pulse: 128 (over y, z, x_hi), rng: 4 (over x_lo, core).
Axes of the slice: x: 4 (x_hi: 2, x_lo: 2; x = x_hi * 2 + x_lo), y: 4, z: 16, core: 2. Of those that a mesh axis runs over, the one named last changes fastest.
Arguments:
- echoes: bfloat16 [2, 16384, 8192], P(None, 'pulse', 'rng'), may hold values from -6 to 6
- range_ref: bfloat16 [2, 1024], replicated, may hold values from -0.125 to 0.125
- band_weights: bfloat16 [64, 8192], P(None, 'rng'), may hold values from -0.75 to 0.75
- band_offsets: int32 [8192], P('rng'), may hold values from 0 to 32, as said below
- azimuth_ref: bfloat16 [2, 512], replicated, may hold values from -0.1875 to 0.1875
Outputs:
- image: float32 [2, 4, 2048, 16384], P(None, 'rng', 'pulse')
Inputs may be any that keep to these rules, and one draw needn't show every extreme that they name: `band_offsets`: every value from 0 to one half of 64 may occur; both ends occur in every draw.
All inputs are finite; a program needn't handle non-finite values.
Results may differ from a plain program's by a relative error of at most 0.0041.
Values may be sent and summed in bfloat16 or wider, within the bound.
A program may use at most 64 MiB of HBM per device.

v0:
```python
import jax
import jax.numpy as jnp
from jax import lax
from jax.sharding import PartitionSpec as P

RT = 1024
AT = 512
BAND = 64
BLK = 128


def from_behind(value, axis, steps):
    count = lax.axis_size(axis)
    first, last = (max(0, -steps), min(count, count - steps))
    return lax.ppermute(value, axis, [(source, source + steps) for source in range(first, last)])


def with_halo(block, sides, width):
    for axis, dim in sides:
        count = lax.axis_size(axis)
        forward = [(i, i + 1) for i in range(count - 1)]
        backward = [(target, source) for source, target in forward]
        low = lax.ppermute(
            lax.slice_in_dim(block, block.shape[dim] - width, None, axis=dim), axis, forward
        )
        high = lax.ppermute(lax.slice_in_dim(block, 0, width, axis=dim), axis, backward)
        block = jnp.concatenate([low, block, high], axis=dim)
    return block


def skew_rows(matrix_rows):
    leading = matrix_rows.shape[:-2]
    row_count = matrix_rows.shape[-2]
    row_length = matrix_rows.shape[-1]
    widths = [(0, 0)] * len(leading) + [(0, 0), (0, row_count)]
    padded = jnp.pad(matrix_rows, widths)
    flattened = padded.reshape(leading + (row_count * (row_length + row_count),))
    kept = flattened[..., : row_count * (row_length + row_count - 1)]
    return kept.reshape(leading + (row_count, row_length + row_count - 1))


def toeplitz_real(filter_taps, block_count):
    tap_total = filter_taps.shape[1]
    span_total = block_count * BLK
    row_length = span_total - BLK + 1
    padded_taps = jnp.pad(filter_taps, ((0, 0), (0, row_length - tap_total)))
    repeated = jnp.broadcast_to(padded_taps[:, None, :], (2, BLK, row_length))
    skewed = skew_rows(repeated)
    skewed_parts = skewed.reshape(2, BLK, block_count, BLK).transpose(0, 2, 3, 1)
    real_part = skewed_parts[0]
    imag_part = skewed_parts[1]
    upper = jnp.stack([real_part, -imag_part], axis=2)
    lower = jnp.stack([imag_part, real_part], axis=2)
    return jnp.stack([upper, lower], axis=1)


def correlate(blocks, kernel, out_blocks):
    running = None
    for tap_block in range(kernel.shape[0]):
        window = blocks[:, :, tap_block : tap_block + out_blocks]
        partial_sum = jnp.einsum(
            "zrbi,ziwc->wrbc", window, kernel[tap_block], preferred_element_type=jnp.float32
        )
        running = partial_sum if running is None else running + partial_sum
    return running


def band_matrices(weights_t, offsets, block_total):
    table = weights_t.reshape(BAND, block_total, BLK).transpose(1, 0, 2)
    reach_rows = BAND + BAND // 2
    placed = jnp.pad(table, ((0, 0), (0, BAND // 2), (0, 0)))
    shifts = offsets.reshape(block_total, 1, BLK)
    for bit_number in range((BAND // 2).bit_length()):
        step_size = 1 << bit_number
        shifted = jnp.pad(placed[:, : reach_rows - step_size], ((0, 0), (step_size, 0), (0, 0)))
        placed = jnp.where(shifts // step_size % 2 == 1, shifted, placed)
    columns = jnp.pad(
        placed.transpose(0, 2, 1), ((0, 0), (0, 0), (BAND // 2, BLK + 1 - BAND // 2 - reach_rows))
    )
    skewed = skew_rows(columns)
    return skewed.transpose(0, 2, 1)


def migrate_padded(padded, weights_t, offsets):
    block_total = offsets.shape[0] // BLK
    matrices = band_matrices(weights_t, offsets, block_total)
    pulse_total = padded.shape[1]
    tiles = padded.reshape(2, pulse_total, block_total + 1, BLK)
    lower = jnp.einsum(
        "zrbi,bic->zbcr", tiles[:, :, :-1], matrices[:, :BLK], preferred_element_type=jnp.float32
    )
    upper = jnp.einsum(
        "zrbi,bic->zbcr", tiles[:, :, 1:], matrices[:, BLK:], preferred_element_type=jnp.float32
    )
    return (lower + upper).reshape(2, block_total * BLK, pulse_total).astype(jnp.bfloat16)


def azimuth_focus(migrated, kernel):
    bin_total = migrated.shape[1]
    pulse_total = migrated.shape[2]
    padded = jnp.pad(migrated, ((0, 0), (0, 0), (AT // 2, AT // 2)))
    blocks = padded.reshape(2, bin_total, (pulse_total + AT) // BLK, BLK)
    return correlate(blocks, kernel, pulse_total // BLK).reshape(2, bin_total, pulse_total)


def per_device(echoes, range_ref, band_weights, band_offsets, azimuth_ref):
    pulse_rows = echoes.shape[1]
    quarter_len = echoes.shape[2]
    block_total = quarter_len // BLK
    range_kernel = toeplitz_real(range_ref, RT // BLK + 1)
    following = from_behind(echoes[:, :, :RT], "rng", -1)
    joined = jnp.concatenate([echoes, following], axis=2)
    blocks = joined.reshape(2, pulse_rows, block_total + RT // BLK, BLK)
    compressed = (
        correlate(blocks, range_kernel, block_total)
        .reshape(2, pulse_rows, quarter_len)
        .astype(jnp.bfloat16)
    )
    padded = with_halo(compressed, (("rng", 2),), BAND)
    migrated = migrate_padded(padded, band_weights, band_offsets)
    pulse_peers = lax.axis_size("pulse")
    grouped = migrated.reshape(2, pulse_peers, quarter_len // pulse_peers, pulse_rows)
    azimuth_kernel = toeplitz_real(azimuth_ref, AT // BLK + 1)
    return azimuth_focus(
        lax.all_to_all(grouped, "pulse", split_axis=1, concat_axis=3, tiled=True)[:, 0],
        azimuth_kernel,
    )[:, None]


def solution(mesh):
    return jax.shard_map(
        per_device,
        mesh=mesh,
        in_specs=(P(None, "pulse", "rng"), P(), P(None, "rng"), P("rng"), P()),
        out_specs=P(None, "rng", "pulse", None),
        check_vma=False,
    )
```

profile of v0, /device:TPU:1, one launch (start us, length us, event | category | flops | bytes accessed | tf_op | source)
XLA Modules:
  0.0 165.6 jit_solution(18233479786403594663)
XLA Ops:
  0.0 1.6 copy.68
  2.5 8.8 %collective-permute-start = (bf16[2,128,1024]{1,2,0:T(8,128)(2,1)}, bf16[2,128,1024]{1,2,0:T(8,128)(2,1)}, u32[]{:S(2)}, u32[]{:S(2)}) collective-permute-start(bf16[2,128,1024]{1,2,0:T(8,128)(2,1)} %slice.209), channel_id=1, source_target_pairs={{1,0},{2,1},{3,2},{5,4},{6,5},{7,6},{9,8},{10,9},{11,10},{13,12},{... | collective-permute-start | bytes 1572872 | tf_op jit(solution)/shard_map/ppermute | solution.py:15
  11.4 1.7 %reshape.457 = bf16[2,147584]{1,0:T(2,128)(2,1)S(1)} reshape(bf16[2,128,1153]{2,1,0:T(8,128)(2,1)S(1)} %pad.68) | data formatting | bytes 1180672 | tf_op jit(solution)/shard_map/reshape | solution.py:37
  17.6 1.3 pad_select_fusion
  20.0 3.1 %fusion.106 = (bf16[2,128,16,128]{1,3,2,0:T(8,128)(2,1)}, bf16[2,128,16,128]{1,3,2,0:T(8,128)(2,1)S(1)}, bf16[2,128,16,128]{1,3,2,0:T(8,128)(2,1)S(1)}, bf16[2,1...) fusion(bf16[2,128,24,128]{1,3,2,0:T(8,128)(2,1)S(1)} %bitcast.306), kind=kLoop, calls=%fused_computation.191 | loop fusion | bytes 18874368 | tf_op jit(solution)/shard_map/slice | solution.py:60
  23.1 1.3 copy.128
  24.5 1.4 copy.127
  25.8 1.8 %fusion.11 = f32[2,128,128,16,1]{2,1,4,3,0:T(8,128)S(1)} fusion(bf16[2,128,16,128]{3,1,0,2:T(8,128)(2,1)} %copy.128, bf16[9,1,128,2,128]{2,4,1,3,0:T(8,128)(2,1)S(1)} %get-tuple-element.28, bf16[9,1,128,2,128]{2,4,1,3,0:T(8,128)(2,1)S(1)} %get-tuple-element.27), kind=kOutput, calls=%fused_computation.47 | convolution fusion | flops 268697600 | bytes 4325376 | tf_op jit(solution)/shard_map/zrbi,ziwc->wrbc/dot_general | solution.py:61
  27.6 1.8 %fusion.13 = f32[2,128,128,16,1]{2,1,4,3,0:T(8,128)} fusion(bf16[2,128,16,128]{3,1,0,2:T(8,128)(2,1)S(1)} %copy-done.3, bf16[9,1,128,2,128]{2,4,1,3,0:T(8,128)(2,1)S(1)} %get-tuple-element.28, bf16[9,1,128,2,128]{2,4,1,3,0:T(8,128)(2,1)S(1)} %get-tuple-element.27), kind=kOutput, calls=%fused_computation.49 | convolution fusion | flops 268697600 | bytes 4325376 | tf_op jit(solution)/shard_map/zrbi,ziwc->wrbc/dot_general | solution.py:61
  29.4 2.3 %copy.126 = bf16[2,128,16,128]{3,1,0,2:T(8,128)(2,1)} copy(bf16[2,128,16,128]{1,3,2,0:T(8,128)(2,1)} %get-tuple-element.8) | data formatting | bytes 2097152
  31.7 3.0 %fusion.15 = f32[2,128,128,16,1]{2,1,4,3,0:T(8,128)} fusion(bf16[2,128,16,128]{3,1,0,2:T(8,128)(2,1)} %copy.126, bf16[9,1,128,2,128]{2,4,1,3,0:T(8,128)(2,1)S(1)} %get-tuple-element.28, bf16[9,1,128,2,128]{2,4,1,3,0:T(8,128)(2,1)S(1)} %get-tuple-element.27), kind=kOutput, calls=%fused_computation.51 | convolution fusion | flops 268697600 | bytes 4325376 | tf_op jit(solution)/shard_map/zrbi,ziwc->wrbc/dot_general | solution.py:61
  34.7 2.3 %copy.125 = bf16[2,128,16,128]{3,1,0,2:T(8,128)(2,1)} copy(bf16[2,128,16,128]{1,3,2,0:T(8,128)(2,1)} %get-tuple-element.9) | data formatting | bytes 2097152
  37.0 3.0 %fusion.17 = f32[2,128,128,16,1]{2,1,4,3,0:T(8,128)} fusion(bf16[2,128,16,128]{3,1,0,2:T(8,128)(2,1)} %copy.125, bf16[9,1,128,2,128]{2,4,1,3,0:T(8,128)(2,1)S(1)} %get-tuple-element.28, bf16[9,1,128,2,128]{2,4,1,3,0:T(8,128)(2,1)S(1)} %get-tuple-element.27), kind=kOutput, calls=%fused_computation.53 | convolution fusion | flops 268697600 | bytes 4325376 | tf_op jit(solution)/shard_map/zrbi,ziwc->wrbc/dot_general | solution.py:61
  40.0 2.3 %copy.124 = bf16[2,128,16,128]{3,1,0,2:T(8,128)(2,1)} copy(bf16[2,128,16,128]{1,3,2,0:T(8,128)(2,1)} %get-tuple-element.10) | data formatting | bytes 2097152
  42.3 3.0 %fusion.19 = f32[2,128,128,16,1]{2,1,4,3,0:T(8,128)} fusion(bf16[2,128,16,128]{3,1,0,2:T(8,128)(2,1)} %copy.124, bf16[9,1,128,2,128]{2,4,1,3,0:T(8,128)(2,1)S(1)} %get-tuple-element.28, bf16[9,1,128,2,128]{2,4,1,3,0:T(8,128)(2,1)S(1)} %get-tuple-element.27), kind=kOutput, calls=%fused_computation.55 | convolution fusion | flops 268697600 | bytes 4325376 | tf_op jit(solution)/shard_map/zrbi,ziwc->wrbc/dot_general | solution.py:61
  45.4 2.3 %copy.123 = bf16[2,128,16,128]{3,1,0,2:T(8,128)(2,1)} copy(bf16[2,128,16,128]{1,3,2,0:T(8,128)(2,1)} %get-tuple-element.11) | data formatting | bytes 2097152
  47.7 3.1 %fusion.21 = f32[2,128,128,16,1]{2,1,4,3,0:T(8,128)} fusion(bf16[2,128,16,128]{3,1,0,2:T(8,128)(2,1)} %copy.123, bf16[9,1,128,2,128]{2,4,1,3,0:T(8,128)(2,1)S(1)} %get-tuple-element.28, bf16[9,1,128,2,128]{2,4,1,3,0:T(8,128)(2,1)S(1)} %get-tuple-element.27), kind=kOutput, calls=%fused_computation.57 | convolution fusion | flops 268697600 | bytes 4325376 | tf_op jit(solution)/shard_map/zrbi,ziwc->wrbc/dot_general | solution.py:61
  50.7 2.3 %copy.122 = bf16[2,128,16,128]{3,1,0,2:T(8,128)(2,1)} copy(bf16[2,128,16,128]{1,3,2,0:T(8,128)(2,1)} %get-tuple-element.12) | data formatting | bytes 2097152
  53.0 3.1 %fusion.23 = f32[2,128,128,16,1]{2,1,4,3,0:T(8,128)} fusion(bf16[2,128,16,128]{3,1,0,2:T(8,128)(2,1)} %copy.122, bf16[9,1,128,2,128]{2,4,1,3,0:T(8,128)(2,1)S(1)} %get-tuple-element.28, bf16[9,1,128,2,128]{2,4,1,3,0:T(8,128)(2,1)S(1)} %get-tuple-element.27), kind=kOutput, calls=%fused_computation.59 | convolution fusion | flops 268697600 | bytes 4325376 | tf_op jit(solution)/shard_map/zrbi,ziwc->wrbc/dot_general | solution.py:61
  56.1 2.3 %copy.121 = bf16[2,128,16,128]{3,1,0,2:T(8,128)(2,1)} copy(bf16[2,128,16,128]{1,3,2,0:T(8,128)(2,1)} %get-tuple-element.13) | data formatting | bytes 2097152
  58.4 3.0 %fusion.25 = f32[2,128,128,16,1]{2,1,4,3,0:T(8,128)} fusion(bf16[2,128,16,128]{3,1,0,2:T(8,128)(2,1)} %copy.121, bf16[9,1,128,2,128]{2,4,1,3,0:T(8,128)(2,1)S(1)} %get-tuple-element.28, bf16[9,1,128,2,128]{2,4,1,3,0:T(8,128)(2,1)S(1)} %get-tuple-element.27), kind=kOutput, calls=%fused_computation.61 | convolution fusion | flops 268697600 | bytes 4325376 | tf_op jit(solution)/shard_map/zrbi,ziwc->wrbc/dot_general | solution.py:61
  61.4 2.3 %copy.129 = bf16[2,128,16,128]{3,1,0,2:T(8,128)(2,1)} copy(bf16[2,128,16,128]{1,3,2,0:T(8,128)(2,1)} %get-tuple-element.5) | data formatting | bytes 2097152
  63.7 6.8 %fusion.1 = bf16[2,128,128,16]{2,1,3,0:T(8,128)(2,1)S(1)} fusion(f32[2,128,128,16,1]{2,1,4,3,0:T(8,128)S(1)} %fusion.11, f32[2,128,128,16,1]{2,1,4,3,0:T(8,128)} %fusion.13, f32[2,128,128,16,1]{2,1,4,3,0:T(8,128)} %fusion.15, f32[2,128,128,16,1]{2,1,4,3,0:T(8,128)} %fusion.17, f32[2,128,128,16,1]{2,1,4,3,0:T(8,128)} %fusion.19, ...), kind=kOutput, calls=%fused_computation.22 | convolution fusion | flops 273416192 | bytes 20054016 | tf_op jit(solution)/shard_map/zrbi,ziwc->wrbc/dot_general | solution.py:61
  70.6 1.9 %collective-permute-start.2 = (bf16[2,128,64]{1,2,0:T(8,128)(2,1)S(1)}, bf16[2,128,64]{1,2,0:T(8,128)(2,1)S(1)}, u32[]{:S(2)}, u32[]{:S(2)}) collective-permute-start(bf16[2,128,64]{1,2,0:T(8,128)(2,1)S(1)} %get-tuple-element.22), channel_id=1, source_target_pairs={{1,0},{2,1},{3,2},{5,4},{6,5},{7,6},{9,8},{10,9},{11,10},{13,12},{... | collective-permute-start | bytes 98312 | tf_op jit(solution)/shard_map/ppermute | solution.py:26
  72.5 3.6 %collective-permute-start.1 = (bf16[2,128,64]{1,2,0:T(8,128)(2,1)S(1)}, bf16[2,128,64]{1,2,0:T(8,128)(2,1)S(1)}, u32[]{:S(2)}, u32[]{:S(2)}) collective-permute-start(bf16[2,128,64]{1,2,0:T(8,128)(2,1)S(1)} %get-tuple-element.21), channel_id=1, source_target_pairs={{0,1},{1,2},{2,3},{4,5},{5,6},{6,7},{8,9},{9,10},{10,11},{12,13},{... | collective-permute-start | bytes 98312 | tf_op jit(solution)/shard_map/ppermute | solution.py:23
  77.1 2.0 %reshape.455 = bf16[16,32896]{1,0:T(8,128)(2,1)S(1)} reshape(bf16[16,128,257]{2,1,0:T(8,128)(2,1)S(1)} %pad.87) | data formatting | bytes 2105344 | tf_op jit(solution)/shard_map/reshape | solution.py:37
  82.1 1.2 copy.81
  83.2 17.3 %all-to-all-start = ((bf16[2,128,16,128]{3,2,0,1:T(8,128)(2,1)}), bf16[2,128,16,128]{3,2,0,1:T(8,128)(2,1)S(1)}, u32[]{:S(2)}, u32[]{:S(2)}) async-start(bf16[2,128,16,128]{3,2,0,1:T(8,128)(2,1)} %copy.81), calls=%async_computation | async-start | bytes 2097152 | tf_op jit(solution)/shard_map/all_to_all | solution.py:125
  102.4 53.0 %all-to-all-done = bf16[2,128,16,128]{3,2,0,1:T(8,128)(2,1)S(1)} async-done(((bf16[2,128,16,128]{3,2,0,1:T(8,128)(2,1)}), bf16[2,128,16,128]{3,2,0,1:T(8,128)(2,1)S(1)}, u32[]{:S(2)}, u32[]{:S(2)}) %all-to-all-start) | async-done | bytes 1048608 | tf_op jit(solution)/shard_map/all_to_all | solution.py:125
  160.1 2.0 %fusion = f32[2,16,128,128]{2,3,1,0:T(8,128)} fusion(f32[2,128,16,128,1]{3,1,4,2,0:T(8,128)S(1)} %fusion.3, f32[2,128,16,128,1]{3,1,4,2,0:T(8,128)S(1)} %fusion.4, f32[2,128,16,128,1]{3,1,4,2,0:T(8,128)S(1)} %fusion.5, f32[2,128,16,128,1]{3,1,4,2,0:T(8,128)S(1)} %fusion.6, bf16[2,16,128,128]{3,2,1,0:T(8,128)(2,1)S(1)} %get-tuple-element.14, ...), kind=kOutput, calls=%fused_computation.17 | convolution fusion | flops 270794752 | bytes 12189696 | tf_op jit(solution)/shard_map/zrbi,ziwc->wrbc/dot_general | solution.py:61
  162.1 1.9 %copy.88 = f32[2,16,128,128]{3,2,1,0:T(8,128)S(1)} copy(f32[2,16,128,128]{2,3,1,0:T(8,128)} %fusion) | data formatting | bytes 4194304 | tf_op jit(solution)/shard_map/add | solution.py:64
  164.1 1.5 broadcast_in_dim_reshape.3
  (66 shorter events, 16.7 us)
Async XLA Ops:
  0.0 11.2 %copy-start.6 = (bf16[2,1024]{1,0:T(2,128)(2,1)S(1)}, bf16[2,1024]{1,0:T(2,128)(2,1)}, u32[]{:S(2)}) copy-start(bf16[2,1024]{1,0:T(2,128)(2,1)} %param.6) | copy-start | bytes 12292
  2.5 16.4 %collective-permute-start = (bf16[2,128,1024]{1,2,0:T(8,128)(2,1)}, bf16[2,128,1024]{1,2,0:T(8,128)(2,1)}, u32[]{:S(2)}, u32[]{:S(2)}) collective-permute-start(bf16[2,128,1024]{1,2,0:T(8,128)(2,1)} %slice.209), channel_id=1, source_target_pairs={{1,0},{2,1},{3,2},{5,4},{6,5},{7,6},{9,8},{10,9},{11,10},{13,12},{... | collective-permute-start | bytes 1572872 | tf_op jit(solution)/shard_map/ppermute | solution.py:15
  14.0 1.0 copy-start.4
  14.2 1.2 copy-start.5
  25.8 1.8 %copy-start.3 = (bf16[2,128,16,128]{3,1,0,2:T(8,128)(2,1)S(1)}, bf16[2,128,16,128]{3,1,0,2:T(8,128)(2,1)}, u32[]{:S(2)}) copy-start(bf16[2,128,16,128]{3,1,0,2:T(8,128)(2,1)} %copy.127) | copy-start | bytes 3145732
  63.7 12.4 %copy-start = (bf16[16,96,128]{1,2,0:T(8,128)(2,1)S(1)}, bf16[16,96,128]{1,2,0:T(8,128)(2,1)}, u32[]{:S(2)}) copy-start(bf16[16,96,128]{1,2,0:T(8,128)(2,1)} %pad_select_fusion) | copy-start | bytes 1179652
  70.5 6.1 %copy-start.1 = (bf16[2,128,128,16]{2,1,3,0:T(8,128)(2,1)}, bf16[2,128,128,16]{2,1,3,0:T(8,128)(2,1)S(1)}, u32[]{:S(2)}) copy-start(bf16[2,128,128,16]{2,1,3,0:T(8,128)(2,1)S(1)} %fusion.1) | copy-start | bytes 3145732
  70.6 8.9 %collective-permute-start.2 = (bf16[2,128,64]{1,2,0:T(8,128)(2,1)S(1)}, bf16[2,128,64]{1,2,0:T(8,128)(2,1)S(1)}, u32[]{:S(2)}, u32[]{:S(2)}) collective-permute-start(bf16[2,128,64]{1,2,0:T(8,128)(2,1)S(1)} %get-tuple-element.22), channel_id=1, source_target_pairs={{1,0},{2,1},{3,2},{5,4},{6,5},{7,6},{9,8},{10,9},{11,10},{13,12},{... | collective-permute-start | bytes 98312 | tf_op jit(solution)/shard_map/ppermute | solution.py:26
  72.5 7.0 %collective-permute-start.1 = (bf16[2,128,64]{1,2,0:T(8,128)(2,1)S(1)}, bf16[2,128,64]{1,2,0:T(8,128)(2,1)S(1)}, u32[]{:S(2)}, u32[]{:S(2)}) collective-permute-start(bf16[2,128,64]{1,2,0:T(8,128)(2,1)S(1)} %get-tuple-element.21), channel_id=1, source_target_pairs={{0,1},{1,2},{2,3},{4,5},{5,6},{6,7},{8,9},{9,10},{10,11},{12,13},{... | collective-permute-start | bytes 98312 | tf_op jit(solution)/shard_map/ppermute | solution.py:23
  79.1 1.2 copy-start.2
  82.0 18.5 %copy-start.7 = (bf16[2,512]{1,0:T(2,128)(2,1)S(1)}, bf16[2,512]{1,0:T(2,128)(2,1)}, u32[]{:S(2)}) copy-start(bf16[2,512]{1,0:T(2,128)(2,1)} %param.9) | copy-start | bytes 6148
  83.2 72.2 %all-to-all-start = ((bf16[2,128,16,128]{3,2,0,1:T(8,128)(2,1)}), bf16[2,128,16,128]{3,2,0,1:T(8,128)(2,1)S(1)}, u32[]{:S(2)}, u32[]{:S(2)}) async-start(bf16[2,128,16,128]{3,2,0,1:T(8,128)(2,1)} %copy.81), calls=%async_computation | async-start | bytes 2097152 | tf_op jit(solution)/shard_map/all_to_all | solution.py:125
where the time goes:
time: 166 us
  waiting for transfers between devices  53 us (32%)
  local copies, waits for them, and re-layouts  41.7 us (25%)
  matrix products  33.4 us (20%)
  starting transfers between devices  31.7 us (19%)
  other arithmetic  5.24 us (3%)
    all_to_all x1, waiting for transfers between devices, per_device(): lax.all_to_all(grouped, 'pulse', split_axis=1, concat_axis=3, tiled=True)  53 us
    dot_general x14, matrix products, correlate(): jnp.einsum('zrbi,ziwc->wrbc', window, kernel[tap_block], preferred_elemen...  32.5 us
    unnamed x27, local copies, waits for them, and re-layouts  22.2 us
    all_to_all x1, starting transfers between devices, per_device(): lax.all_to_all(grouped, 'pulse', split_axis=1, concat_axis=3, tiled=True)  17.3 us
    ppermute x1, starting transfers between devices, from_behind(): lax.ppermute(value, axis, [(source, source + steps) for source in range(f...  8.78 us
    reshape x3, local copies, waits for them, and re-layouts, skew_rows(): padded.reshape(leading + (row_count * (row_length + row_count),))  4.79 us
    slice x2, local copies, waits for them, and re-layouts, correlate(): window = blocks[:, :, tap_block:tap_block + out_blocks]  4.26 us
    ppermute x1, starting transfers between devices, with_halo(): lax.ppermute(lax.slice_in_dim(block, block.shape[dim] - width, None, axis...  3.64 us
  transfers between devices with their start and end apart: 4, of which 1 were waited for; matrix products, arithmetic and copies ran while one was open for 7% of the time, Pallas kernels for 0%

commit v1 on v0

v1 whole, which is shorter than its diff:
```python
import jax
import jax.numpy as jnp
from jax import lax
from jax.experimental import pallas as pl
from jax.experimental.pallas import tpu as pltpu
from jax.sharding import PartitionSpec as P

MESH = pl.DeviceIdType.MESH
BLK = 128
PAIR = 2 * BLK
VMEM_BYTES = 40 * 1024 * 1024


def place_toeplitz(taps_ref, rows_ref, turned_ref, matrix_ref):
    chunks = taps_ref.shape[1] // BLK
    rows_ref[...] = jnp.zeros_like(rows_ref)
    for k in range(chunks):
        chunk = taps_ref[:, k * BLK : (k + 1) * BLK].astype(jnp.float32)
        rows_ref[2 * k : 2 * k + 2, BLK:PAIR] = chunk
        rows_ref[2 * k + 2 : 2 * k + 4, 0:BLK] = chunk
    source = lax.broadcasted_iota(jnp.int32, (PAIR, PAIR), 0)
    lane = lax.broadcasted_iota(jnp.int32, (PAIR, PAIR), 1)
    wanted = jnp.where(lane < BLK, BLK - lane, 3 * BLK - lane)
    turn = jnp.where(source == wanted, 1.0, 0.0).astype(jnp.bfloat16)
    turned_ref[...] = jnp.dot(
        rows_ref[...].astype(jnp.bfloat16), turn, preferred_element_type=jnp.float32
    )
    for k in range(chunks + 1):
        tiles = []
        for part in range(2):
            row = turned_ref[2 * k + part : 2 * k + part + 1, :]
            spread = jnp.broadcast_to(row, (BLK, PAIR))
            tiles.append(pltpu.roll(spread, 0, 1, stride=1, stride_axis=0)[:, :BLK])
        real, imag = tiles
        top = k * PAIR
        matrix_ref[top : top + BLK, 0:BLK] = real.astype(jnp.bfloat16)
        matrix_ref[top : top + BLK, BLK:PAIR] = (-imag).astype(jnp.bfloat16)
        matrix_ref[top + BLK : top + PAIR, 0:BLK] = imag.astype(jnp.bfloat16)
        matrix_ref[top + BLK : top + PAIR, BLK:PAIR] = real.astype(jnp.bfloat16)


def compress_kernel(
    pulse_peers,
    quarters,
    echoes,
    range_ref,
    weights,
    offsets,
    azimuth_ref,
    gathered,
    azimuth_matrix,
    own,
    right_halo,
    left_halo,
    joined,
    range_rows,
    range_turned,
    range_matrix,
    azimuth_rows,
    azimuth_turned,
    azimuth_held,
    compressed,
    outgoing,
    own_sem,
    halo_send_sem,
    halo_recv_sem,
    send_sem,
    recv_sem,
    local_sem,
    matrix_sem,
):
    me = lax.axis_index("pulse")
    quarter = lax.axis_index("rng")
    quarter_len = own.shape[2]
    blocks = quarter_len // BLK
    taps_blocks = range_ref.shape[1] // BLK
    depth = range_matrix.shape[0]
    has_right = quarter < quarters - 1
    has_left = quarter > 0

    barrier = pltpu.get_barrier_semaphore()

    @pl.when(has_right)
    def _():
        pl.semaphore_signal(barrier, inc=1, device_id=(me, quarter + 1), device_id_type=MESH)

    @pl.when(has_left)
    def _():
        pl.semaphore_signal(barrier, inc=1, device_id=(me, quarter - 1), device_id_type=MESH)

    def greet(step, carry):
        peer = lax.rem(me + step, pulse_peers)
        pl.semaphore_signal(barrier, inc=1, device_id=(peer, quarter), device_id_type=MESH)
        return carry

    lax.fori_loop(1, pulse_peers, greet, 0)

    load = pltpu.make_async_copy(echoes, own, own_sem)
    load.start()
    place_toeplitz(range_ref, range_rows, range_turned, range_matrix)
    load.wait()

    def join(source, first, count):
        for m in range(count):
            for part in range(2):
                at = (first + m) * PAIR + part * BLK
                joined[:, at : at + BLK] = source[part, :, m * BLK : (m + 1) * BLK]

    join(own, 1, blocks)

    neighbours = jnp.where(has_right, 1, 0) + jnp.where(has_left, 1, 0)
    pl.semaphore_wait(barrier, pulse_peers - 1 + neighbours)

    reach = right_halo.shape[2]
    to_left = pltpu.make_async_remote_copy(
        src_ref=echoes.at[:, :, pl.ds(0, reach)],
        dst_ref=right_halo,
        send_sem=halo_send_sem.at[0],
        recv_sem=halo_recv_sem.at[0],
        device_id=(me, quarter - 1),
        device_id_type=MESH,
    )
    to_right = pltpu.make_async_remote_copy(
        src_ref=echoes.at[:, :, pl.ds(quarter_len - BLK, BLK)],
        dst_ref=left_halo,
        send_sem=halo_send_sem.at[1],
        recv_sem=halo_recv_sem.at[1],
        device_id=(me, quarter + 1),
        device_id_type=MESH,
    )

    @pl.when(has_left)
    def _():
        to_left.start()

    @pl.when(has_right)
    def _():
        to_right.start()

    def compress(j):
        window = joined[:, pl.ds(pl.multiple_of((j + 1) * PAIR, PAIR), depth)]
        block = jnp.dot(window, range_matrix[...], preferred_element_type=jnp.float32)
        top = pl.multiple_of((j + 1) * BLK, BLK)
        compressed[pl.ds(top, BLK), 0:BLK] = block[:, 0:BLK].T.astype(jnp.bfloat16)
        compressed[pl.ds(top, BLK), BLK:PAIR] = block[:, BLK:PAIR].T.astype(jnp.bfloat16)

    def migrate(b):
        taps = weights.shape[0]
        table = weights[:, pl.ds(pl.multiple_of(b * BLK, BLK), BLK)].astype(jnp.float32)
        shift_row = offsets[pl.ds(b, 1), :].astype(jnp.float32)
        stacked = jnp.concatenate(
            [table, jnp.broadcast_to(shift_row, (BLK - taps, BLK))], axis=0
        ).T
        lane = lax.broadcasted_iota(jnp.int32, (BLK, BLK), 1)
        placed = jnp.where(lane < taps, stacked, 0.0)
        shifts = jnp.broadcast_to(stacked[:, taps : taps + 1], (BLK, BLK)).astype(jnp.int32)
        step = 1
        while step <= taps // 2:
            moved = pltpu.roll(placed, step, 1)
            placed = jnp.where((shifts & step) != 0, moved, placed)
            step *= 2
        wide = jnp.concatenate([placed, jnp.zeros_like(placed)], axis=1)
        band = pltpu.roll(wide, taps // 2, 1, stride=1, stride_axis=0).astype(jnp.bfloat16)
        top = pl.multiple_of(b * BLK + BLK // 2, BLK // 2)
        moved = jnp.dot(
            band, compressed[pl.ds(top, PAIR), :], preferred_element_type=jnp.float32
        ).astype(jnp.bfloat16)
        bins = outgoing.shape[2]
        peers = BLK // bins
        first = b * peers
        for part in range(2):
            outgoing[pl.ds(first, peers), part] = moved[:, part * BLK : (part + 1) * BLK].reshape(
                peers, bins, BLK
            )

        def send(n, carry):
            peer = first + n

            @pl.when(peer != me)
            def _():
                pltpu.make_async_remote_copy(
                    src_ref=outgoing.at[peer],
                    dst_ref=gathered.at[me],
                    send_sem=send_sem,
                    recv_sem=recv_sem,
                    device_id=(peer, quarter),
                    device_id_type=MESH,
                ).start()

            return carry

        lax.fori_loop(0, peers, send, 0)

    compress(0)
    compress(1)

    def inner(j, carry):
        compress(j)
        migrate(j - 1)
        return carry

    inner_end = blocks - taps_blocks
    lax.fori_loop(2, inner_end, inner, 0)

    @pl.when(has_left)
    def _():
        to_right.wait_recv()

    @pl.when(has_right)
    def _():
        to_left.wait_recv()

    @pl.when(jnp.logical_not(has_right))
    def _():
        right_halo[...] = jnp.zeros_like(right_halo)

    join(right_halo, blocks + 1, reach // BLK)

    @pl.when(has_left)
    def _():
        join(left_halo, 0, 1)
        compress(-1)

    @pl.when(jnp.logical_not(has_left))
    def _():
        compressed[0:BLK, :] = jnp.zeros((BLK, PAIR), jnp.bfloat16)

    migrate(0)
    lax.fori_loop(inner_end, blocks + 1, inner, 0)

    keep = pltpu.make_async_copy(outgoing.at[me], gathered.at[me], local_sem)
    keep.start()
    place_toeplitz(azimuth_ref, azimuth_rows, azimuth_turned, azimuth_held)
    store = pltpu.make_async_copy(azimuth_held, azimuth_matrix, matrix_sem)
    store.start()

    @pl.when(has_left)
    def _():
        to_left.wait_send()

    @pl.when(has_right)
    def _():
        to_right.wait_send()

    keep.wait()
    store.wait()
    others = pl.ds(0, pulse_peers - 1)
    pltpu.make_async_copy(outgoing.at[others], gathered.at[others], send_sem).wait()
    pltpu.make_async_copy(outgoing.at[others], gathered.at[others], recv_sem).wait()


def focus_kernel(gathered, matrix, image, padded):
    step = pl.program_id(0)
    sources = gathered.shape[0]
    bins = gathered.shape[2]
    reach = matrix.shape[0] // PAIR
    edge = (reach - 1) // 2 * bins

    @pl.when(step == 0)
    def _():
        padded[0:edge, :] = jnp.zeros((edge, PAIR), jnp.bfloat16)
        padded[edge + sources * bins :, :] = jnp.zeros((edge, PAIR), jnp.bfloat16)
        for part in range(2):
            padded[edge : edge + sources * bins, part * BLK : (part + 1) * BLK] = gathered[
                :, part
            ].reshape(sources * bins, BLK)

    count = image.shape[3] // BLK
    top = pl.multiple_of(step * count * bins, bins)
    window = jnp.concatenate(
        [padded[pl.ds(pl.multiple_of(top + k * bins, bins), count * bins), :] for k in range(reach)],
        axis=1,
    )
    focused = jnp.dot(window, matrix[...], preferred_element_type=jnp.float32)
    for n in range(count):
        for part in range(2):
            image[part, 0, :, n * BLK : (n + 1) * BLK] = focused[
                n * bins : (n + 1) * bins, part * BLK : (part + 1) * BLK
            ]


def per_device(echoes, range_ref, band_weights, band_offsets, azimuth_ref):
    pulse_peers = lax.axis_size("pulse")
    quarters = lax.axis_size("rng")
    pulse_rows = echoes.shape[1]
    quarter_len = echoes.shape[2]
    blocks = quarter_len // BLK
    bins = quarter_len // pulse_peers
    range_blocks = range_ref.shape[1] // BLK
    azimuth_blocks = azimuth_ref.shape[1] // BLK
    reach = (range_blocks + 1) * BLK
    range_pad = -(-(2 * range_blocks + 2) // 8) * 8
    azimuth_pad = -(-(2 * azimuth_blocks + 2) // 8) * 8
    range_depth = (range_blocks + 1) * PAIR
    azimuth_depth = (azimuth_blocks + 1) * PAIR
    anywhere = pl.BlockSpec(memory_space=pl.ANY)
    in_vmem = pl.BlockSpec(memory_space=pltpu.VMEM)

    def kernel(*refs):
        compress_kernel(pulse_peers, quarters, *refs)

    gathered, matrix = pl.pallas_call(
        kernel,
        out_shape=(
            jax.ShapeDtypeStruct((pulse_peers, 2, bins, pulse_rows), jnp.bfloat16),
            jax.ShapeDtypeStruct((azimuth_depth, PAIR), jnp.bfloat16),
        ),
        in_specs=[anywhere, in_vmem, in_vmem, in_vmem, in_vmem],
        out_specs=(anywhere, anywhere),
        scratch_shapes=[
            pltpu.VMEM((2, pulse_rows, quarter_len), jnp.bfloat16),
            pltpu.VMEM((2, pulse_rows, reach), jnp.bfloat16),
            pltpu.VMEM((2, pulse_rows, BLK), jnp.bfloat16),
            pltpu.VMEM((pulse_rows, (blocks + 1 + reach // BLK) * PAIR), jnp.bfloat16),
            pltpu.VMEM((range_pad, PAIR), jnp.float32),
            pltpu.VMEM((range_pad, PAIR), jnp.float32),
            pltpu.VMEM((range_depth, PAIR), jnp.bfloat16),
            pltpu.VMEM((azimuth_pad, PAIR), jnp.float32),
            pltpu.VMEM((azimuth_pad, PAIR), jnp.float32),
            pltpu.VMEM((azimuth_depth, PAIR), jnp.bfloat16),
            pltpu.VMEM(((blocks + 2) * BLK, PAIR), jnp.bfloat16),
            pltpu.VMEM((pulse_peers, 2, bins, pulse_rows), jnp.bfloat16),
            pltpu.SemaphoreType.DMA,
            pltpu.SemaphoreType.DMA((2,)),
            pltpu.SemaphoreType.DMA((2,)),
            pltpu.SemaphoreType.DMA,
            pltpu.SemaphoreType.DMA,
            pltpu.SemaphoreType.DMA,
            pltpu.SemaphoreType.DMA,
        ],
        compiler_params=pltpu.CompilerParams(
            collective_id=0, has_side_effects=True, vmem_limit_bytes=VMEM_BYTES
        ),
        name="compress_and_exchange",
    )(echoes, range_ref, band_weights, band_offsets.reshape(blocks, BLK), azimuth_ref)

    steps = 8
    pulses = pulse_peers * pulse_rows
    return pl.pallas_call(
        focus_kernel,
        out_shape=jax.ShapeDtypeStruct((2, 1, bins, pulses), jnp.float32),
        grid=(steps,),
        in_specs=[
            pl.BlockSpec((pulse_peers, 2, bins, pulse_rows), lambda s: (0, 0, 0, 0)),
            pl.BlockSpec((azimuth_depth, PAIR), lambda s: (0, 0)),
        ],
        out_specs=pl.BlockSpec((2, 1, bins, pulses // steps), lambda s: (0, 0, 0, s)),
        scratch_shapes=[
            pltpu.VMEM(((pulse_peers + azimuth_blocks) * bins, PAIR), jnp.bfloat16)
        ],
        compiler_params=pltpu.CompilerParams(vmem_limit_bytes=VMEM_BYTES),
        name="focus",
    )(gathered, matrix)


def solution(mesh):
    return jax.shard_map(
        per_device,
        mesh=mesh,
        in_specs=(P(None, "pulse", "rng"), P(), P(None, "rng"), P("rng"), P()),
        out_specs=P(None, "rng", "pulse", None),
        check_vma=False,
    )
```

time: 166 us -> 77.9 us (0.47)
  the two profiles are of different devices: /device:TPU:1 before, /device:TPU:62 now
where the time goes in v1:
time: 77.9 us; the launch traced here: 77.7 us
  Pallas kernels  73.4 us (94%)
  local copies, waits for them, and re-layouts  4.24 us (5%)
    pallas_call x1, Pallas kernels, per_device(): pl.pallas_call(kernel, out_shape=(jax.ShapeDtypeStruct((pulse_peers, 2, b...  68.6 us
    pallas_call x1, Pallas kernels, per_device(): pl.pallas_call(focus_kernel, out_shape=jax.ShapeDtypeStruct((2, 1, bins,...  4.75 us
    unnamed x10, local copies, waits for them, and re-layouts  4.24 us

profile of v1, /device:TPU:62, one launch (start us, length us, event | category | flops | bytes accessed | tf_op | source)
XLA Modules:
  0.0 77.7 jit_solution(2699947754345888134)
XLA Ops:
  0.0 0.0 copy-start
  0.0 1.2 %copy-done = bf16[2,128,2048]{2,1,0:T(8,128)(2,1)S(1)} copy-done((bf16[2,128,2048]{2,1,0:T(8,128)(2,1)S(1)}, bf16[2,128,2048]{2,1,0:T(8,128)(2,1)}, u32[]{:S(2)}) %copy-start) | copy-done | bytes 1048600
  1.2 0.0 copy-start.1
  1.2 0.9 %copy-done.1 = bf16[64,2048]{1,0:T(8,128)(2,1)S(1)} copy-done((bf16[64,2048]{1,0:T(8,128)(2,1)S(1)}, bf16[64,2048]{1,0:T(8,128)(2,1)}, u32[]{:S(2)}) %copy-start.1) | copy-done | bytes 262168
  2.2 0.0 copy-start.2
  2.2 0.7 copy-done.2
  2.9 0.0 copy-start.3
  2.9 0.7 copy-done.3
  3.6 0.0 copy-start.4
  3.6 0.7 copy-done.4
  4.2 68.6 %compress_and_exchange.1 = (bf16[128,2,16,128]{3,2,1,0:T(8,128)(2,1)S(1)}, bf16[1280,256]{1,0:T(8,128)(2,1)S(1)}) custom-call(bf16[2,128,2048]{2,1,0:T(8,128)(2,1)S(1)} %copy-done, bf16[2,1024]{1,0:T(2,128)(2,1)S(1)} %copy-done.3, bf16[64,2048]{1,0:T(8,128)(2,1)S(1)} %copy-done.1, s32[16,128]{1,0:T(8,128)S(1)} %bitcast.1, bf16[2,512]{1,0:T(2,128)(2,1)S(1)} %copy-done.4), custom_call_target="tpu_custom_call" | custom-call | tf_op jit(solution)/shard_map/compress_and_exchange/pallas_call | solution.py:302
  72.9 4.8 %focus.1 = f32[2,1,16,16384]{3,2,1,0:T(8,128)} custom-call(bf16[128,2,16,128]{3,2,1,0:T(8,128)(2,1)S(1)} %get-tuple-element.7.gathered, bf16[1280,256]{1,0:T(8,128)(2,1)S(1)} %get-tuple-element.8.matrix), custom_call_target="tpu_custom_call" | custom-call | tf_op jit(solution)/shard_map/focus/pallas_call | solution.py:339
Async XLA Ops:
  0.0 1.2 %copy-start = (bf16[2,128,2048]{2,1,0:T(8,128)(2,1)S(1)}, bf16[2,128,2048]{2,1,0:T(8,128)(2,1)}, u32[]{:S(2)}) copy-start(bf16[2,128,2048]{2,1,0:T(8,128)(2,1)} %refs_0_.1) | copy-start | bytes 3145732
  1.2 0.9 %copy-start.1 = (bf16[64,2048]{1,0:T(8,128)(2,1)S(1)}, bf16[64,2048]{1,0:T(8,128)(2,1)}, u32[]{:S(2)}) copy-start(bf16[64,2048]{1,0:T(8,128)(2,1)} %refs_2_.1) | copy-start | bytes 786436
  2.2 0.7 copy-start.2
  2.9 0.7 copy-start.3
  3.6 0.7 copy-start.4

commit v2 on v1

v2 whole, which is shorter than its diff:
```python
import jax
import jax.numpy as jnp
from jax import lax
from jax.experimental import pallas as pl
from jax.experimental.pallas import tpu as pltpu
from jax.sharding import PartitionSpec as P

MESH = pl.DeviceIdType.MESH
BLK = 128
PAIR = 2 * BLK
VMEM_BYTES = 56 * 1024 * 1024


def place_toeplitz(taps_ref, rows_ref, turned_ref, matrix_ref):
    chunks = taps_ref.shape[1] // BLK
    rows_ref[...] = jnp.zeros_like(rows_ref)
    for k in range(chunks):
        chunk = taps_ref[:, k * BLK : (k + 1) * BLK].astype(jnp.float32)
        rows_ref[2 * k : 2 * k + 2, BLK:PAIR] = chunk
        rows_ref[2 * k + 2 : 2 * k + 4, 0:BLK] = chunk
    source = lax.broadcasted_iota(jnp.int32, (PAIR, PAIR), 0)
    lane = lax.broadcasted_iota(jnp.int32, (PAIR, PAIR), 1)
    wanted = jnp.where(lane < BLK, BLK - lane, 3 * BLK - lane)
    turn = jnp.where(source == wanted, 1.0, 0.0).astype(jnp.bfloat16)
    turned_ref[...] = jnp.dot(
        rows_ref[...].astype(jnp.bfloat16), turn, preferred_element_type=jnp.float32
    )
    for k in range(chunks + 1):
        tiles = []
        for part in range(2):
            row = turned_ref[2 * k + part : 2 * k + part + 1, :]
            spread = jnp.broadcast_to(row, (BLK, PAIR))
            tiles.append(pltpu.roll(spread, 0, 1, stride=1, stride_axis=0)[:, :BLK])
        real, imag = tiles
        top = k * PAIR
        matrix_ref[top : top + BLK, 0:BLK] = real.astype(jnp.bfloat16)
        matrix_ref[top : top + BLK, BLK:PAIR] = (-imag).astype(jnp.bfloat16)
        matrix_ref[top + BLK : top + PAIR, 0:BLK] = imag.astype(jnp.bfloat16)
        matrix_ref[top + BLK : top + PAIR, BLK:PAIR] = real.astype(jnp.bfloat16)


def focus_whole(
    pulse_peers,
    quarters,
    echoes_hbm,
    range_hbm,
    weights_hbm,
    offsets_hbm,
    azimuth_hbm,
    image,
    own,
    right_halo,
    left_halo,
    range_ref,
    weights,
    offsets,
    azimuth_ref,
    joined,
    range_rows,
    range_turned,
    range_matrix,
    azimuth_rows,
    azimuth_turned,
    azimuth_matrix,
    compressed,
    outgoing,
    gathered,
    focused,
    load_sem,
    halo_send_sem,
    halo_recv_sem,
    send_sem,
    recv_sem,
    local_sem,
    image_sem,
):
    me = lax.axis_index("pulse")
    quarter = lax.axis_index("rng")
    pulse_rows = own.shape[1]
    quarter_len = own.shape[2]
    blocks = quarter_len // BLK
    range_steps = range_matrix.shape[0] // PAIR
    azimuth_steps = azimuth_matrix.shape[0] // PAIR
    taps = weights.shape[0]
    bins = outgoing.shape[2]
    peers = BLK // bins
    groups = recv_sem.shape[0]
    group = pulse_peers // groups
    edge = (azimuth_steps - 1) // 2
    has_right = quarter < quarters - 1
    has_left = quarter > 0

    barrier = pltpu.get_barrier_semaphore()

    loads = [
        pltpu.make_async_copy(source, target, load_sem.at[n])
        for n, (source, target) in enumerate(
            (
                (range_hbm, range_ref),
                (echoes_hbm, own),
                (weights_hbm, weights),
                (offsets_hbm, offsets),
                (azimuth_hbm, azimuth_ref),
            )
        )
    ]
    for load in loads:
        load.start()

    @pl.when(has_right)
    def _():
        pl.semaphore_signal(barrier, inc=1, device_id=(me, quarter + 1), device_id_type=MESH)

    @pl.when(has_left)
    def _():
        pl.semaphore_signal(barrier, inc=1, device_id=(me, quarter - 1), device_id_type=MESH)

    def greet(step, carry):
        peer = lax.rem(me + step, pulse_peers)
        pl.semaphore_signal(barrier, inc=1, device_id=(peer, quarter), device_id_type=MESH)
        return carry

    lax.fori_loop(1, pulse_peers, greet, 0)

    loads[0].wait()
    place_toeplitz(range_ref, range_rows, range_turned, range_matrix)
    for load in loads[1:]:
        load.wait()

    def join(source, first, count):
        for m in range(count):
            for part in range(2):
                joined[
                    (first + m) * pulse_rows : (first + m + 1) * pulse_rows,
                    part * BLK : (part + 1) * BLK,
                ] = source[part, :, m * BLK : (m + 1) * BLK]

    join(own, 1, blocks)

    def compress(*js):
        window = jnp.concatenate(
            [
                jnp.concatenate(
                    [
                        joined[
                            pl.ds(pl.multiple_of((j + 1 + k) * pulse_rows, pulse_rows), pulse_rows)
                        ]
                        for j in js
                    ],
                    axis=0,
                )
                for k in range(range_steps)
            ],
            axis=1,
        )
        block = jnp.dot(window, range_matrix[...], preferred_element_type=jnp.float32)
        block = block.astype(jnp.bfloat16)
        for n, j in enumerate(js):
            at = pl.ds(pl.multiple_of((j + 1) * BLK, BLK), BLK)
            for part in range(2):
                compressed[part * pulse_rows : (part + 1) * pulse_rows, at] = block[
                    n * pulse_rows : (n + 1) * pulse_rows, part * BLK : (part + 1) * BLK
                ]

    def band_of(b):
        start = BLK - BLK // 2 + taps // 2
        lane = lax.broadcasted_iota(jnp.int32, (8, BLK), 1)
        shift = jnp.broadcast_to(offsets[pl.ds(b, 1), :], (8, BLK)) + lane

        def shifted(bit, rows):
            return jnp.concatenate([(shift & bit) != 0] * (rows // 8), axis=0)

        table = weights[:, pl.ds(pl.multiple_of(b * BLK, BLK), BLK)].astype(jnp.float32)
        placed = jnp.concatenate([table, jnp.zeros((8, BLK), jnp.float32)], axis=0)
        for bit in (1, 2, 4):
            rows = placed.shape[0]
            placed = jnp.where(shifted(bit, rows), pltpu.roll(placed, bit, 0), placed)
        bit = 8
        while bit <= BLK - 1 + taps // 2:
            blank = jnp.zeros((bit, BLK), jnp.float32)
            lower = jnp.concatenate([blank, placed], axis=0)
            upper = jnp.concatenate([placed, blank], axis=0)
            placed = jnp.where(shifted(bit, lower.shape[0]), lower, upper)
            bit *= 2
        return jnp.concatenate(
            [jnp.zeros((start, BLK), jnp.float32), placed[: 3 * BLK - start]], axis=0
        ).astype(jnp.bfloat16)

    def migrate(b):
        around = compressed[:, pl.ds(pl.multiple_of(b * BLK, BLK), 3 * BLK)]
        moved = jnp.dot(around, band_of(b), preferred_element_type=jnp.float32)
        for part in range(2):
            turned = moved[part * pulse_rows : (part + 1) * pulse_rows].T.astype(jnp.bfloat16)
            outgoing[pl.ds(b * peers, peers), part] = turned.reshape(peers, bins, pulse_rows)

    def send(b):
        def one(n, carry):
            peer = b * peers + n

            @pl.when(peer != me)
            def _():
                pltpu.make_async_remote_copy(
                    src_ref=outgoing.at[peer],
                    dst_ref=gathered.at[me + edge],
                    send_sem=send_sem,
                    recv_sem=recv_sem.at[me // group],
                    device_id=(peer, quarter),
                    device_id_type=MESH,
                ).start()

            return carry

        lax.fori_loop(0, peers, one, 0)

    half = blocks - range_steps + 1
    compress(0, 1)

    def first_pairs(i, carry):
        compress(2 * i, 2 * i + 1)
        migrate(2 * i - 1)
        migrate(2 * i)
        return carry

    lax.fori_loop(1, half // 2, first_pairs, 0)

    neighbours = jnp.where(has_right, 1, 0) + jnp.where(has_left, 1, 0)
    pl.semaphore_wait(barrier, pulse_peers - 1 + neighbours)

    reach = right_halo.shape[2]
    to_left = pltpu.make_async_remote_copy(
        src_ref=own.at[:, :, pl.ds(0, reach)],
        dst_ref=right_halo,
        send_sem=halo_send_sem.at[0],
        recv_sem=halo_recv_sem.at[0],
        device_id=(me, quarter - 1),
        device_id_type=MESH,
    )
    to_right = pltpu.make_async_remote_copy(
        src_ref=own.at[:, :, pl.ds(quarter_len - BLK, BLK)],
        dst_ref=left_halo,
        send_sem=halo_send_sem.at[1],
        recv_sem=halo_recv_sem.at[1],
        device_id=(me, quarter + 1),
        device_id_type=MESH,
    )

    @pl.when(has_left)
    def _():
        to_left.start()

    @pl.when(has_right)
    def _():
        to_right.start()

    def send_first(b, carry):
        send(b)
        return carry

    lax.fori_loop(1, half - 1, send_first, 0)

    place_toeplitz(azimuth_ref, azimuth_rows, azimuth_turned, azimuth_matrix)
    gathered[0:edge] = jnp.zeros((edge,) + gathered.shape[1:], jnp.bfloat16)
    gathered[edge + pulse_peers :] = jnp.zeros((edge,) + gathered.shape[1:], jnp.bfloat16)

    @pl.when(has_left)
    def _():
        to_right.wait_recv()
        join(left_halo, 0, 1)

    @pl.when(has_right)
    def _():
        to_left.wait_recv()
        join(right_halo, blocks + 1, reach // BLK)

    @pl.when(jnp.logical_not(has_left))
    def _():
        joined[0:pulse_rows, :] = jnp.zeros((pulse_rows, PAIR), jnp.bfloat16)

    @pl.when(jnp.logical_not(has_right))
    def _():
        rest = reach // BLK * pulse_rows
        joined[(blocks + 1) * pulse_rows :, :] = jnp.zeros((rest, PAIR), jnp.bfloat16)

    compress(-1, half)

    @pl.when(jnp.logical_not(has_left))
    def _():
        compressed[:, 0:BLK] = jnp.zeros((2 * pulse_rows, BLK), jnp.bfloat16)

    migrate(0)
    send(0)
    migrate(half - 1)
    send(half - 1)

    def second_pairs(i, carry):
        j = half + 1 + 2 * i
        compress(j, j + 1)
        migrate(j - 1)
        send(j - 1)
        migrate(j)
        send(j)
        return carry

    lax.fori_loop(0, (blocks - half) // 2, second_pairs, 0)

    keep = pltpu.make_async_copy(outgoing.at[me], gathered.at[me + edge], local_sem)
    keep.start()
    keep.wait()

    def arrive(g):
        for count, mine in ((group - 1, True), (group, False)):

            @pl.when((me // group == g) == mine)
            def _():
                pltpu.make_async_copy(
                    outgoing.at[pl.ds(0, count)], gathered.at[pl.ds(edge, count)], recv_sem.at[g]
                ).wait()

    def put(g):
        lanes = pl.ds(pl.multiple_of(g * group * BLK, BLK), group * BLK)
        return pltpu.make_async_copy(
            focused.at[:, :, :, lanes], image.at[:, :, :, lanes], image_sem
        )

    def focus(g, carry):
        @pl.when(g < groups - 1)
        def _():
            arrive(g + 1)

        window = jnp.concatenate(
            [
                gathered[pl.ds(g * group + k, group), part].reshape(group * bins, pulse_rows)
                for k in range(azimuth_steps)
                for part in range(2)
            ],
            axis=1,
        )
        result = jnp.dot(window, azimuth_matrix[...], preferred_element_type=jnp.float32)
        for n in range(group):
            at = pl.ds(pl.multiple_of((g * group + n) * BLK, BLK), BLK)
            for part in range(2):
                focused[part, 0, :, at] = result[
                    n * bins : (n + 1) * bins, part * BLK : (part + 1) * BLK
                ]
        put(g).start()
        return carry

    arrive(0)
    lax.fori_loop(0, groups, focus, 0)

    @pl.when(has_left)
    def _():
        to_left.wait_send()

    @pl.when(has_right)
    def _():
        to_right.wait_send()

    others = pl.ds(0, pulse_peers - 1)
    pltpu.make_async_copy(outgoing.at[others], gathered.at[others], send_sem).wait()
    pltpu.make_async_copy(focused, image, image_sem).wait()


def place_image(source, image, held, load_sem, store_sem):
    count = load_sem.shape[0]
    width = image.shape[3] // count
    stores = []
    loads = []
    for n in range(count):
        lanes = pl.ds(n * width, width)
        load = pltpu.make_async_copy(
            source.at[:, :, :, lanes], held.at[:, :, :, lanes], load_sem.at[n]
        )
        load.start()
        loads.append(load)
    for n in range(count):
        lanes = pl.ds(n * width, width)
        loads[n].wait()
        store = pltpu.make_async_copy(
            held.at[:, :, :, lanes], image.at[:, :, :, lanes], store_sem.at[n]
        )
        store.start()
        stores.append(store)
    for store in stores:
        store.wait()


def per_device(echoes, range_ref, band_weights, band_offsets, azimuth_ref):
    pulse_peers = lax.axis_size("pulse")
    quarters = lax.axis_size("rng")
    pulse_rows = echoes.shape[1]
    quarter_len = echoes.shape[2]
    blocks = quarter_len // BLK
    bins = quarter_len // pulse_peers
    range_blocks = range_ref.shape[1] // BLK
    azimuth_blocks = azimuth_ref.shape[1] // BLK
    reach = (range_blocks + 1) * BLK
    range_pad = -(-(2 * range_blocks + 2) // 8) * 8
    azimuth_pad = -(-(2 * azimuth_blocks + 2) // 8) * 8
    range_depth = (range_blocks + 1) * PAIR
    azimuth_depth = (azimuth_blocks + 1) * PAIR
    pulses = pulse_peers * pulse_rows
    groups = 16
    anywhere = pl.BlockSpec(memory_space=pl.ANY)
    bf16 = jnp.bfloat16
    f32 = jnp.float32
    image_shape = (2, 1, bins, pulses)

    def kernel(*refs):
        focus_whole(pulse_peers, quarters, *refs)

    image = pl.pallas_call(
        kernel,
        out_shape=jax.ShapeDtypeStruct(image_shape, f32),
        in_specs=[anywhere] * 5,
        out_specs=anywhere,
        scratch_shapes=[
            pltpu.VMEM((2, pulse_rows, quarter_len), bf16),
            pltpu.VMEM((2, pulse_rows, reach), bf16),
            pltpu.VMEM((2, pulse_rows, BLK), bf16),
            pltpu.VMEM(range_ref.shape, bf16),
            pltpu.VMEM(band_weights.shape, bf16),
            pltpu.VMEM((blocks, BLK), jnp.int32),
            pltpu.VMEM(azimuth_ref.shape, bf16),
            pltpu.VMEM(((blocks + 1 + reach // BLK) * pulse_rows, PAIR), bf16),
            pltpu.VMEM((range_pad, PAIR), f32),
            pltpu.VMEM((range_pad, PAIR), f32),
            pltpu.VMEM((range_depth, PAIR), bf16),
            pltpu.VMEM((azimuth_pad, PAIR), f32),
            pltpu.VMEM((azimuth_pad, PAIR), f32),
            pltpu.VMEM((azimuth_depth, PAIR), bf16),
            pltpu.VMEM((2 * pulse_rows, (blocks + 2) * BLK), bf16),
            pltpu.VMEM((pulse_peers, 2, bins, pulse_rows), bf16),
            pltpu.VMEM((pulse_peers + azimuth_blocks, 2, bins, pulse_rows), bf16),
            pltpu.VMEM(image_shape, f32),
            pltpu.SemaphoreType.DMA((5,)),
            pltpu.SemaphoreType.DMA((2,)),
            pltpu.SemaphoreType.DMA((2,)),
            pltpu.SemaphoreType.DMA,
            pltpu.SemaphoreType.DMA((groups,)),
            pltpu.SemaphoreType.DMA,
            pltpu.SemaphoreType.DMA,
        ],
        compiler_params=pltpu.CompilerParams(
            collective_id=0, has_side_effects=True, vmem_limit_bytes=VMEM_BYTES
        ),
        name="focus_whole",
    )(echoes, range_ref, band_weights, band_offsets.reshape(blocks, BLK), azimuth_ref)

    pieces = 4
    return pl.pallas_call(
        place_image,
        out_shape=jax.ShapeDtypeStruct(image_shape, f32),
        in_specs=[anywhere],
        out_specs=anywhere,
        scratch_shapes=[
            pltpu.VMEM(image_shape, f32),
            pltpu.SemaphoreType.DMA((pieces,)),
            pltpu.SemaphoreType.DMA((pieces,)),
        ],
        compiler_params=pltpu.CompilerParams(vmem_limit_bytes=VMEM_BYTES),
        name="place_image",
    )(image)


def solution(mesh):
    return jax.shard_map(
        per_device,
        mesh=mesh,
        in_specs=(P(None, "pulse", "rng"), P(), P(None, "rng"), P("rng"), P()),
        out_specs=P(None, "rng", "pulse", None),
        check_vma=False,
    )
```

time: 77.9 us -> 72.4 us (0.929)
  the two profiles are of different devices: /device:TPU:62 before, /device:TPU:29 now
where the time goes in v2:
time: 72.4 us; the launch traced here: 72.3 us
  Pallas kernels  72.2 us (100%)
    pallas_call x1, Pallas kernels, per_device(): pl.pallas_call(kernel, out_shape=jax.ShapeDtypeStruct(image_shape, f32),...  69.8 us
    pallas_call x1, Pallas kernels, per_device(): pl.pallas_call(place_image, out_shape=jax.ShapeDtypeStruct(image_shape, f...  2.42 us

profile of v2, /device:TPU:29, one launch (start us, length us, event | category | flops | bytes accessed | tf_op | source)
XLA Modules:
  0.0 72.3 jit_solution(3880851072405282559)
XLA Ops:
  0.0 69.8 %focus_whole.1.source = f32[2,1,16,16384]{3,2,1,0:T(8,128)} custom-call(bf16[2,128,2048]{2,1,0:T(8,128)(2,1)} %refs_0_.1, bf16[2,1024]{1,0:T(2,128)(2,1)} %refs_1_.1, bf16[64,2048]{1,0:T(8,128)(2,1)} %refs_2_.1, s32[16,128]{1,0:T(8,128)} %bitcast.1, bf16[2,512]{1,0:T(2,128)(2,1)} %refs_4_.1), custom_call_target="tpu_custom_call" | custom-call | tf_op jit(solution)/shard_map/focus_whole/pallas_call | solution.py:412
  69.8 2.4 %place_image.1 = f32[2,1,16,16384]{3,2,1,0:T(8,128)} custom-call(f32[2,1,16,16384]{3,2,1,0:T(8,128)} %focus_whole.1.source), custom_call_target="tpu_custom_call" | custom-call | tf_op jit(solution)/shard_map/place_image/pallas_call | solution.py:451

commit v3 on v2

--- a/solution.py
+++ b/solution.py
@@ -8,7 +8,7 @@
 MESH = pl.DeviceIdType.MESH
 BLK = 128
 PAIR = 2 * BLK
-VMEM_BYTES = 56 * 1024 * 1024
+VMEM_BYTES = 44 * 1024 * 1024
 
 
 def place_toeplitz(taps_ref, rows_ref, turned_ref, matrix_ref):
@@ -65,14 +65,12 @@
     compressed,
     outgoing,
     gathered,
-    focused,
     load_sem,
     halo_send_sem,
     halo_recv_sem,
     send_sem,
     recv_sem,
     local_sem,
-    image_sem,
 ):
     me = lax.axis_index("pulse")
     quarter = lax.axis_index("rng")
@@ -252,11 +250,14 @@
     def _():
         to_right.start()
 
+    stride = blocks // 4
+    send(stride)
+
     def send_first(b, carry):
         send(b)
         return carry
 
-    lax.fori_loop(1, half - 1, send_first, 0)
+    lax.fori_loop(1, stride, send_first, 0)
 
     place_toeplitz(azimuth_ref, azimuth_rows, azimuth_turned, azimuth_matrix)
     gathered[0:edge] = jnp.zeros((edge,) + gathered.shape[1:], jnp.bfloat16)
@@ -289,19 +290,26 @@
 
     migrate(0)
     send(0)
-    migrate(half - 1)
-    send(half - 1)
 
     def second_pairs(i, carry):
         j = half + 1 + 2 * i
         compress(j, j + 1)
-        migrate(j - 1)
-        send(j - 1)
-        migrate(j)
-        send(j)
         return carry
 
     lax.fori_loop(0, (blocks - half) // 2, second_pairs, 0)
+
+    def late(u, carry):
+        b = half + u // 2 + stride * (u % 2)
+        migrate(b)
+        send(b)
+        return carry
+
+    lax.fori_loop(0, 2, late, 0)
+    lax.fori_loop(stride + 1, half - 1, send_first, 0)
+    lax.fori_loop(2, 6, late, 0)
+    migrate(half - 1)
+    send(half - 1)
+    lax.fori_loop(6, 8, late, 0)
 
     keep = pltpu.make_async_copy(outgoing.at[me], gathered.at[me + edge], local_sem)
     keep.start()
@@ -315,12 +323,6 @@
                 pltpu.make_async_copy(
                     outgoing.at[pl.ds(0, count)], gathered.at[pl.ds(edge, count)], recv_sem.at[g]
                 ).wait()
-
-    def put(g):
-        lanes = pl.ds(pl.multiple_of(g * group * BLK, BLK), group * BLK)
-        return pltpu.make_async_copy(
-            focused.at[:, :, :, lanes], image.at[:, :, :, lanes], image_sem
-        )
 
     def focus(g, carry):
         @pl.when(g < groups - 1)
@@ -339,10 +341,9 @@
         for n in range(group):
             at = pl.ds(pl.multiple_of((g * group + n) * BLK, BLK), BLK)
             for part in range(2):
-                focused[part, 0, :, at] = result[
+                image[part, 0, :, at] = result[
                     n * bins : (n + 1) * bins, part * BLK : (part + 1) * BLK
                 ]
-        put(g).start()
         return carry
 
     arrive(0)
@@ -358,31 +359,12 @@
 
     others = pl.ds(0, pulse_peers - 1)
     pltpu.make_async_copy(outgoing.at[others], gathered.at[others], send_sem).wait()
-    pltpu.make_async_copy(focused, image, image_sem).wait()
-
-
-def place_image(source, image, held, load_sem, store_sem):
-    count = load_sem.shape[0]
-    width = image.shape[3] // count
-    stores = []
-    loads = []
-    for n in range(count):
-        lanes = pl.ds(n * width, width)
-        load = pltpu.make_async_copy(
-            source.at[:, :, :, lanes], held.at[:, :, :, lanes], load_sem.at[n]
-        )
-        load.start()
-        loads.append(load)
-    for n in range(count):
-        lanes = pl.ds(n * width, width)
-        loads[n].wait()
-        store = pltpu.make_async_copy(
-            held.at[:, :, :, lanes], image.at[:, :, :, lanes], store_sem.at[n]
-        )
-        store.start()
-        stores.append(store)
-    for store in stores:
-        store.wait()
+
+
+def place_image(source, image, sem):
+    copy = pltpu.make_async_copy(source, image, sem)
+    copy.start()
+    copy.wait()
 
 
 def per_device(echoes, range_ref, band_weights, band_offsets, azimuth_ref):
@@ -400,8 +382,9 @@
     range_depth = (range_blocks + 1) * PAIR
     azimuth_depth = (azimuth_blocks + 1) * PAIR
     pulses = pulse_peers * pulse_rows
-    groups = 16
+    groups = 8
     anywhere = pl.BlockSpec(memory_space=pl.ANY)
+    in_vmem = pl.BlockSpec(memory_space=pltpu.VMEM)
     bf16 = jnp.bfloat16
     f32 = jnp.float32
     image_shape = (2, 1, bins, pulses)
@@ -413,7 +396,7 @@
         kernel,
         out_shape=jax.ShapeDtypeStruct(image_shape, f32),
         in_specs=[anywhere] * 5,
-        out_specs=anywhere,
+        out_specs=in_vmem,
         scratch_shapes=[
             pltpu.VMEM((2, pulse_rows, quarter_len), bf16),
             pltpu.VMEM((2, pulse_rows, reach), bf16),
@@ -432,32 +415,36 @@
             pltpu.VMEM((2 * pulse_rows, (blocks + 2) * BLK), bf16),
             pltpu.VMEM((pulse_peers, 2, bins, pulse_rows), bf16),
             pltpu.VMEM((pulse_peers + azimuth_blocks, 2, bins, pulse_rows), bf16),
-            pltpu.VMEM(image_shape, f32),
             pltpu.SemaphoreType.DMA((5,)),
             pltpu.SemaphoreType.DMA((2,)),
             pltpu.SemaphoreType.DMA((2,)),
             pltpu.SemaphoreType.DMA,
             pltpu.SemaphoreType.DMA((groups,)),
             pltpu.SemaphoreType.DMA,
-            pltpu.SemaphoreType.DMA,
         ],
         compiler_params=pltpu.CompilerParams(
             collective_id=0, has_side_effects=True, vmem_limit_bytes=VMEM_BYTES
         ),
         name="focus_whole",
-    )(echoes, range_ref, band_weights, band_offsets.reshape(blocks, BLK), azimuth_ref)
-
-    pieces = 4
+    )(
+        *(
+            pltpu.with_memory_space_constraint(operand, pltpu.HBM)
+            for operand in (
+                echoes,
+                range_ref,
+                band_weights,
+                band_offsets.reshape(blocks, BLK),
+                azimuth_ref,
+            )
+        )
+    )
+
     return pl.pallas_call(
         place_image,
         out_shape=jax.ShapeDtypeStruct(image_shape, f32),
-        in_specs=[anywhere],
+        in_specs=[in_vmem],
         out_specs=anywhere,
-        scratch_shapes=[
-            pltpu.VMEM(image_shape, f32),
-            pltpu.SemaphoreType.DMA((pieces,)),
-            pltpu.SemaphoreType.DMA((pieces,)),
-        ],
+        scratch_shapes=[pltpu.SemaphoreType.DMA],
         compiler_params=pltpu.CompilerParams(vmem_limit_bytes=VMEM_BYTES),
         name="place_image",
     )(image)

time: 72.4 us -> 68.3 us (0.943)
  the two profiles are of different devices: /device:TPU:29 before, /device:TPU:157 now
where the time goes in v3:
time: 68.3 us; the launch traced here: 68.2 us
  Pallas kernels  68.2 us (100%)
    pallas_call x1, Pallas kernels, per_device(): pl.pallas_call(kernel, out_shape=jax.ShapeDtypeStruct(image_shape, f32),...  66.9 us

profile of v3, /device:TPU:157, one launch (start us, length us, event | category | flops | bytes accessed | tf_op | source)
XLA Modules:
  0.0 68.2 jit_solution(8079312605314089889)
XLA Ops:
  0.0 66.9 %focus_whole.1.source = f32[2,1,16,16384]{3,2,1,0:T(8,128)S(1)} custom-call(bf16[2,128,2048]{2,1,0:T(8,128)(2,1)} %refs_0_.1, bf16[2,1024]{1,0:T(2,128)(2,1)} %refs_1_.1, bf16[64,2048]{1,0:T(8,128)(2,1)} %refs_2_.1, s32[16,128]{1,0:T(8,128)} %bitcast.1, bf16[2,512]{1,0:T(2,128)(2,1)} %refs_4_.1), custom_call_target="tpu_custom_call" | custom-call | tf_op jit(solution)/shard_map/focus_whole/pallas_call | solution.py:395
  66.9 1.3 %place_image.1 = f32[2,1,16,16384]{3,2,1,0:T(8,128)} custom-call(f32[2,1,16,16384]{3,2,1,0:T(8,128)S(1)} %focus_whole.1.source), custom_call_target="tpu_custom_call" | custom-call | tf_op jit(solution)/shard_map/place_image/pallas_call | solution.py:442

commit v4 on v3

--- a/solution.py
+++ b/solution.py
@@ -211,15 +211,11 @@
         lax.fori_loop(0, peers, one, 0)
 
     half = blocks - range_steps + 1
-    compress(0, 1)
-
-    def first_pairs(i, carry):
-        compress(2 * i, 2 * i + 1)
-        migrate(2 * i - 1)
-        migrate(2 * i)
-        return carry
-
-    lax.fori_loop(1, half // 2, first_pairs, 0)
+    stride = blocks // 4
+    compress(stride - 2, stride - 1)
+    compress(stride, stride + 1)
+    migrate(stride)
+    migrate(stride - 1)
 
     neighbours = jnp.where(has_right, 1, 0) + jnp.where(has_left, 1, 0)
     pl.semaphore_wait(barrier, pulse_peers - 1 + neighbours)
@@ -250,15 +246,17 @@
     def _():
         to_right.start()
 
-    stride = blocks // 4
     send(stride)
-
-    def send_first(b, carry):
+    send(stride - 1)
+    compress(0, 1)
+
+    def first(b, carry):
+        migrate(b)
         send(b)
         return carry
 
-    lax.fori_loop(1, stride, send_first, 0)
-
+    lax.fori_loop(1, stride - 1, first, 0)
+    compress(half - 2, half - 1)
     place_toeplitz(azimuth_ref, azimuth_rows, azimuth_turned, azimuth_matrix)
     gathered[0:edge] = jnp.zeros((edge,) + gathered.shape[1:], jnp.bfloat16)
     gathered[edge + pulse_peers :] = jnp.zeros((edge,) + gathered.shape[1:], jnp.bfloat16)
@@ -305,7 +303,7 @@
         return carry
 
     lax.fori_loop(0, 2, late, 0)
-    lax.fori_loop(stride + 1, half - 1, send_first, 0)
+    lax.fori_loop(stride + 1, half - 1, first, 0)
     lax.fori_loop(2, 6, late, 0)
     migrate(half - 1)
     send(half - 1)
@@ -324,30 +322,43 @@
                     outgoing.at[pl.ds(0, count)], gathered.at[pl.ds(edge, count)], recv_sem.at[g]
                 ).wait()
 
-    def focus(g, carry):
-        @pl.when(g < groups - 1)
-        def _():
-            arrive(g + 1)
-
+    def focus(start, count):
         window = jnp.concatenate(
             [
-                gathered[pl.ds(g * group + k, group), part].reshape(group * bins, pulse_rows)
+                gathered[pl.ds(start + k, count), part].reshape(count * bins, pulse_rows)
                 for k in range(azimuth_steps)
                 for part in range(2)
             ],
             axis=1,
         )
         result = jnp.dot(window, azimuth_matrix[...], preferred_element_type=jnp.float32)
-        for n in range(group):
-            at = pl.ds(pl.multiple_of((g * group + n) * BLK, BLK), BLK)
+        for n in range(count):
+            at = pl.ds(pl.multiple_of((start + n) * BLK, BLK), BLK)
             for part in range(2):
                 image[part, 0, :, at] = result[
                     n * bins : (n + 1) * bins, part * BLK : (part + 1) * BLK
                 ]
-        return carry
-
-    arrive(0)
-    lax.fori_loop(0, groups, focus, 0)
+
+    parity = me // group % 2
+    even = parity == 0
+    pairs = groups // 2
+
+    def near(i, carry):
+        g = 2 * i + parity
+        arrive(g)
+        focus(g * group + edge, group - 2 * edge)
+        return carry
+
+    def far(i, carry):
+        g = 2 * i + 1 - parity
+        arrive(g)
+        over = jnp.where(even, jnp.where(i == pairs - 1, edge, 0), jnp.where(i == 0, -edge, 0))
+        focus(g * group - edge - over, group + 2 * edge)
+        return carry
+
+    lax.fori_loop(0, pairs, near, 0)
+    focus(jnp.where(even, 0, pulse_peers - 2 * edge), 2 * edge)
+    lax.fori_loop(0, pairs, far, 0)
 
     @pl.when(has_left)
     def _():

time: 68.3 us -> 67.1 us (0.982)
  the two profiles are of different devices: /device:TPU:157 before, /device:TPU:153 now
where the time goes in v4:
time: 67.1 us; the launch traced here: 67 us
  Pallas kernels  67 us (100%)
    pallas_call x1, Pallas kernels, per_device(): pl.pallas_call(kernel, out_shape=jax.ShapeDtypeStruct(image_shape, f32),...  65.7 us

profile of v4, /device:TPU:153, one launch (start us, length us, event | category | flops | bytes accessed | tf_op | source)
XLA Modules:
  0.0 67.0 jit_solution(14121518116819622676)
XLA Ops:
  0.0 65.7 %focus_whole.1.source = f32[2,1,16,16384]{3,2,1,0:T(8,128)S(1)} custom-call(bf16[2,128,2048]{2,1,0:T(8,128)(2,1)} %refs_0_.1, bf16[2,1024]{1,0:T(2,128)(2,1)} %refs_1_.1, bf16[64,2048]{1,0:T(8,128)(2,1)} %refs_2_.1, s32[16,128]{1,0:T(8,128)} %bitcast.1, bf16[2,512]{1,0:T(2,128)(2,1)} %refs_4_.1), custom_call_target="tpu_custom_call" | custom-call | tf_op jit(solution)/shard_map/focus_whole/pallas_call | solution.py:406
  65.7 1.3 %place_image.1 = f32[2,1,16,16384]{3,2,1,0:T(8,128)} custom-call(f32[2,1,16,16384]{3,2,1,0:T(8,128)S(1)} %focus_whole.1.source), custom_call_target="tpu_custom_call" | custom-call | tf_op jit(solution)/shard_map/place_image/pallas_call | solution.py:453

commit v5 on v4

--- a/solution.py
+++ b/solution.py
@@ -113,12 +113,20 @@
     def _():
         pl.semaphore_signal(barrier, inc=1, device_id=(me, quarter - 1), device_id_type=MESH)
 
-    def greet(step, carry):
+    def greet_one(step):
         peer = lax.rem(me + step, pulse_peers)
         pl.semaphore_signal(barrier, inc=1, device_id=(peer, quarter), device_id_type=MESH)
-        return carry
-
-    lax.fori_loop(1, pulse_peers, greet, 0)
+
+    run = 8
+
+    def greet(turn, carry):
+        for n in range(run):
+            greet_one(turn * run + n + 1)
+        return carry
+
+    lax.fori_loop(0, (pulse_peers - 1) // run, greet, 0)
+    for step in range((pulse_peers - 1) // run * run + 1, pulse_peers):
+        greet_one(step)
 
     loads[0].wait()
     place_toeplitz(range_ref, range_rows, range_turned, range_matrix)
@@ -215,7 +223,6 @@
     compress(stride - 2, stride - 1)
     compress(stride, stride + 1)
     migrate(stride)
-    migrate(stride - 1)
 
     neighbours = jnp.where(has_right, 1, 0) + jnp.where(has_left, 1, 0)
     pl.semaphore_wait(barrier, pulse_peers - 1 + neighbours)
@@ -247,6 +254,7 @@
         to_right.start()
 
     send(stride)
+    migrate(stride - 1)
     send(stride - 1)
     compress(0, 1)
 

time: 67.1 us -> 66.8 us (level)
  no operation moved by 1% of the time
where the time goes in v5:
time: 66.8 us; the launch traced here: 66.7 us
  Pallas kernels  66.7 us (100%)
    pallas_call x1, Pallas kernels, per_device(): pl.pallas_call(kernel, out_shape=jax.ShapeDtypeStruct(image_shape, f32),...  65.4 us

profile of v5, /device:TPU:153, one launch (start us, length us, event | category | flops | bytes accessed | tf_op | source)
XLA Modules:
  0.0 66.7 jit_solution(1188715392387872191)
XLA Ops:
  0.0 65.4 %focus_whole.1.source = f32[2,1,16,16384]{3,2,1,0:T(8,128)S(1)} custom-call(bf16[2,128,2048]{2,1,0:T(8,128)(2,1)} %refs_0_.1, bf16[2,1024]{1,0:T(2,128)(2,1)} %refs_1_.1, bf16[64,2048]{1,0:T(8,128)(2,1)} %refs_2_.1, s32[16,128]{1,0:T(8,128)} %bitcast.1, bf16[2,512]{1,0:T(2,128)(2,1)} %refs_4_.1), custom_call_target="tpu_custom_call" | custom-call | tf_op jit(solution)/shard_map/focus_whole/pallas_call | solution.py:414
  65.4 1.3 %place_image.1 = f32[2,1,16,16384]{3,2,1,0:T(8,128)} custom-call(f32[2,1,16,16384]{3,2,1,0:T(8,128)S(1)} %focus_whole.1.source), custom_call_target="tpu_custom_call" | custom-call | tf_op jit(solution)/shard_map/place_image/pallas_call | solution.py:461

commit v6 on v5

--- a/solution.py
+++ b/solution.py
@@ -233,7 +233,7 @@
         dst_ref=right_halo,
         send_sem=halo_send_sem.at[0],
         recv_sem=halo_recv_sem.at[0],
-        device_id=(me, quarter - 1),
+        device_id=(me, lax.rem(quarter + quarters - 1, quarters)),
         device_id_type=MESH,
     )
     to_right = pltpu.make_async_remote_copy(
@@ -241,7 +241,7 @@
         dst_ref=left_halo,
         send_sem=halo_send_sem.at[1],
         recv_sem=halo_recv_sem.at[1],
-        device_id=(me, quarter + 1),
+        device_id=(me, lax.rem(quarter + 1, quarters)),
         device_id_type=MESH,
     )
 

time: 66.8 us -> 66.8 us (level)
  no operation moved by 1% of the time
where the time goes in v6:
time: 66.8 us; the launch traced here: 66.7 us
  Pallas kernels  66.7 us (100%)
    pallas_call x1, Pallas kernels, per_device(): pl.pallas_call(kernel, out_shape=jax.ShapeDtypeStruct(image_shape, f32),...  65.4 us

profile of v6, /device:TPU:153, one launch (start us, length us, event | category | flops | bytes accessed | tf_op | source)
XLA Modules:
  0.0 66.7 jit_solution(2792647625253427636)
XLA Ops:
  0.0 65.4 %focus_whole.1.source = f32[2,1,16,16384]{3,2,1,0:T(8,128)S(1)} custom-call(bf16[2,128,2048]{2,1,0:T(8,128)(2,1)} %refs_0_.1, bf16[2,1024]{1,0:T(2,128)(2,1)} %refs_1_.1, bf16[64,2048]{1,0:T(8,128)(2,1)} %refs_2_.1, s32[16,128]{1,0:T(8,128)} %bitcast.1, bf16[2,512]{1,0:T(2,128)(2,1)} %refs_4_.1), custom_call_target="tpu_custom_call" | custom-call | tf_op jit(solution)/shard_map/focus_whole/pallas_call | solution.py:414
  65.4 1.3 %place_image.1 = f32[2,1,16,16384]{3,2,1,0:T(8,128)} custom-call(f32[2,1,16,16384]{3,2,1,0:T(8,128)S(1)} %focus_whole.1.source), custom_call_target="tpu_custom_call" | custom-call | tf_op jit(solution)/shard_map/place_image/pallas_call | solution.py:461
